TPU v7x, 32 devices: a whole 2x2x4 slice. The times are simulated.
32 devices in a mesh: group: 2 (over y), expert: 16 (over z, x, core), tensor: 1.
Axes of the slice: x: 2, y: 2, z: 4, core: 2. Of those that a mesh axis runs over, the one named last changes fastest.
Arguments:
- residual: bfloat16 [2048, 3584], P(('group', 'expert', 'tensor')), parts along dimension 0, may hold values from -6 to 6
- head_partials: bfloat16 [1, 2048, 3584], P('tensor', ('group', 'expert')), parts along dimension 1, may hold values from -6 to 6
- norm_gain: float32 [3584], replicated, may hold values from 0.1 to 1.9
- router_weight: float32 [3584, 16], replicated, as said below
- routes: int32 [2048, 8], P(('group', 'expert', 'tensor')), parts along dimension 0, may hold values from 0 to 15, all different within a row; in each aligned block of 64 rows (0 to 63, 64 to 127, ...) at most 48 rows name the same one
- expert_gate: bfloat16 [16, 3584, 1024], P('expert', None, 'tensor'), may hold values from -0.09375 to 0.09375
- expert_up: bfloat16 [16, 3584, 1024], P('expert', None, 'tensor'), may hold values from -0.09375 to 0.09375
- expert_down: bfloat16 [16, 1024, 3584], P('expert', 'tensor'), may hold values from -0.1875 to 0.1875
Outputs:
- mixed: bfloat16 [2048, 3584], P(('group', 'expert', 'tensor')), parts along dimension 0
There are 2 independent parts, one for each index of `group`. A program takes and returns all parts, laid end to end along the dimension named above; an argument that names none is the same for every part. Nothing has to cross between parts.
Inputs may be any that keep to these rules, and one draw needn't show every extreme that they name: `routes`: each node names 8 different experts. Among the 64 nodes of one device no expert is named by more than 48 nodes, and in some devices' nodes one expert is named by exactly 48. `router_weight`: independent entries, each within 2 / sqrt(3584) of zero.
All inputs are finite; a program needn't handle non-finite values.
Results may differ from a plain program's by a relative error of at most 0.019.
Values may be sent and summed in bfloat16 or wider, within the bound.
A program may use at most 128 MiB of HBM per device.

v0:
```python
import jax
import jax.numpy as jnp
from jax import lax
from jax.experimental import pallas as pl
from jax.experimental.pallas import tpu as pltpu
from jax.sharding import PartitionSpec as P

QBLOCK = 128


epsilon = 1e-06
scale_limit = 448.0
route_scale = 2.5


def prepare(residual, attention, norm_gain):
    stream = (residual.astype(jnp.float32) + attention).astype(jnp.bfloat16)
    values = stream.astype(jnp.float32)
    normed = (
        values * lax.rsqrt(jnp.mean(values * values, axis=-1, keepdims=True) + epsilon) * norm_gain
    )
    return (stream, normed)


def quantize(normed, block_size):
    row_count = normed.shape[0]
    blocks = normed.reshape(row_count, -1, block_size)
    scales = ((jnp.max(jnp.abs(blocks), axis=-1) + epsilon) / scale_limit).astype(jnp.bfloat16)
    payload = (blocks / scales.astype(jnp.float32)[:, :, None]).astype(jnp.bfloat16)
    return (payload.reshape(row_count, -1), scales)


def dequantize(payload, scales):
    row_count = payload.shape[0]
    block_size = payload.shape[1] // scales.shape[1]
    blocks = payload.astype(jnp.float32).reshape(row_count, scales.shape[1], block_size)
    blocks = blocks * scales.astype(jnp.float32)[:, :, None]
    return blocks.reshape(row_count, -1).astype(jnp.bfloat16)


def route_weights(normed, router_weight, routes):
    logits = jnp.dot(
        normed, router_weight, precision=lax.Precision.HIGHEST, preferred_element_type=jnp.float32
    )
    affinity = jax.nn.sigmoid(logits)
    labels = jnp.arange(affinity.shape[1], dtype=jnp.int32)
    picked = jnp.sum(
        jnp.where(
            routes[:, :, None] == labels[None, None, :], affinity[:, None, :], jnp.float32(0.0)
        ),
        axis=-1,
    )
    return route_scale * picked / jnp.sum(picked, axis=1, keepdims=True)


def routed(
    residual, head_partials, norm_gain, router_weight, routes, expert_gate, expert_up, expert_down
):
    tensor_count = lax.axis_size("tensor")
    expert_count = lax.axis_size("expert")
    row_count = residual.shape[0]
    top_count = routes.shape[1]
    capacity = max(2, min(row_count, 3 * row_count * top_count // (2 * expert_count)))
    attention = lax.psum_scatter(
        head_partials[0].astype(jnp.float32).astype(jnp.bfloat16),
        "tensor",
        scatter_dimension=0,
        tiled=True,
    ).astype(jnp.float32)
    stream, normed = prepare(residual, attention, norm_gain)
    payload, scales = quantize(normed, QBLOCK)
    weights = route_weights(normed, router_weight, routes)
    pair_count = row_count * top_count
    flat_routes = routes.reshape(pair_count)
    onehot = (flat_routes[:, None] == jnp.arange(expert_count, dtype=jnp.int32)[None, :]).astype(
        jnp.bfloat16
    )
    pair_index = jnp.arange(pair_count, dtype=jnp.int32)
    lower = (pair_index[:, None] > pair_index[None, :]).astype(jnp.bfloat16)
    ahead = jnp.dot(lower, onehot, preferred_element_type=jnp.float32)
    position = jnp.sum(ahead * onehot.astype(jnp.float32), axis=1).astype(jnp.int32)
    slot = flat_routes * capacity + position
    slot_index = jnp.arange(expert_count * capacity, dtype=jnp.int32)
    place = (slot_index[:, None] == slot[None, :]).astype(jnp.bfloat16)
    place_rows = jnp.sum(place.reshape(expert_count * capacity, row_count, top_count), axis=2)
    send_payload = jnp.dot(place_rows, payload, preferred_element_type=jnp.float32).astype(
        jnp.bfloat16
    )
    send_payload = send_payload.reshape(expert_count, capacity, -1)
    send_scales = jnp.dot(place_rows, scales, preferred_element_type=jnp.float32).astype(
        jnp.bfloat16
    )
    send_scales = send_scales.reshape(expert_count, capacity, -1)
    doubled_payload = jnp.repeat(send_payload, tensor_count, axis=0)
    doubled_scales = jnp.repeat(send_scales, tensor_count, axis=0)
    arriving = lax.all_to_all(
        doubled_payload, ("expert", "tensor"), split_axis=0, concat_axis=0, tiled=True
    )
    arriving_scales = lax.all_to_all(
        doubled_scales, ("expert", "tensor"), split_axis=0, concat_axis=0, tiled=True
    )
    sources = arriving.shape[0]
    slots = arriving.shape[1]
    inputs = dequantize(
        arriving.reshape(sources * slots, -1), arriving_scales.reshape(sources * slots, -1)
    )
    gate_part = jnp.dot(inputs, expert_gate[0], preferred_element_type=jnp.float32)
    up_part = jnp.dot(inputs, expert_up[0], preferred_element_type=jnp.float32)
    activated = (jax.nn.silu(gate_part) * up_part).astype(jnp.bfloat16)
    partial_value = jnp.dot(activated, expert_down[0], preferred_element_type=jnp.float32).astype(
        jnp.bfloat16
    )
    partial_value = partial_value.reshape(sources, slots, -1)
    back = lax.all_to_all(
        partial_value, ("expert", "tensor"), split_axis=0, concat_axis=0, tiled=True
    )
    paired = back.reshape(expert_count, tensor_count, back.shape[1], back.shape[2])
    returned = jnp.sum(paired.astype(jnp.float32), axis=1).astype(jnp.bfloat16)
    flat_return = returned.reshape(expert_count * capacity, -1)
    pair_out = jnp.dot(place.T, flat_return, preferred_element_type=jnp.float32)
    moe_sum = jnp.sum(pair_out.reshape(row_count, top_count, -1) * weights[:, :, None], axis=1)
    return (stream.astype(jnp.float32) + moe_sum).astype(jnp.bfloat16)


LAYERS = 4


def pick(table, z):
    value = table[0]
    for i in range(1, LAYERS):
        value = value + (table[i] - table[i - 1]) * ((z + LAYERS - i) // LAYERS)
    return value


def spread_weights(weights, routes, expert_count):
    labels = jnp.arange(expert_count, dtype=jnp.int32)
    return jnp.sum(
        jnp.where(routes[:, :, None] == labels[None, None, :], weights[:, :, None], 0.0), axis=1
    )


def split_three(value):
    first = lax.reduce_precision(value, 8, 7)
    second = lax.reduce_precision(value - first, 8, 7)
    third = value - first - second
    return jnp.concatenate([first, second, third], axis=1).astype(jnp.bfloat16)


def layer_kernel(
    own_ref, stream_ref, gate_hbm, up_hbm, down_hbm, out_ref,
    rows, parts, from_core, from_x, from_z, hidden, gate, up, down,
    send_up, send_dn, send_x, send_core, got_rows,
    back_core, back_x, back_z, got_core, got_x, got_z, weight_sem,
):
    n, width = stream_ref.shape
    full = own_ref.shape[1]
    inner = hidden.shape[1]
    experts = LAYERS * 4
    me = lax.axis_index("expert")
    z, x, c = me // 4, (me // 2) % 2, me % 2
    core_dev = me + 1 - 2 * c
    x_dev = me + 2 - 4 * x
    up_dev, dn_dev = me + 4, me - 4

    def block(layer, xx, cc):
        return layer * 4 + xx * 2 + cc

    def span(b):
        return pl.ds(pl.multiple_of(b * n, n), n)

    barrier = pltpu.get_barrier_semaphore()

    def greet(dev):
        pl.semaphore_signal(
            barrier, inc=1, device_id={"expert": dev}, device_id_type=pl.DeviceIdType.MESH
        )

    greet(core_dev)
    greet(x_dev)
    pl.when(z > 0)(lambda: greet(dn_dev))
    pl.when(z < LAYERS - 1)(lambda: greet(up_dev))

    loads = [
        pltpu.make_async_copy(src.at[0], dst, weight_sem.at[i])
        for i, (src, dst) in enumerate(((gate_hbm, gate), (up_hbm, up), (down_hbm, down)))
    ]
    for load in loads:
        load.start()
    pl.semaphore_wait(barrier, 2 + (z + LAYERS - 1) // LAYERS + (2 * LAYERS - 2 - z) // LAYERS)

    def remote(src, dst, ssem, rsem, dev):
        return pltpu.make_async_remote_copy(
            src_ref=src, dst_ref=dst, send_sem=ssem, recv_sem=rsem,
            device_id={"expert": dev}, device_id_type=pl.DeviceIdType.MESH,
        )

    def row_copy(b, sems, dev, src=None):
        return remote(
            rows.at[span(b)] if src is None else src,
            rows.at[span(b)], sems.at[b], got_rows.at[b], dev,
        )

    def arrived(b):
        row_copy(b, send_core, core_dev).wait_recv()

    row_copy(me, send_x, x_dev, own_ref).start()
    pl.when(z > 0)(lambda: row_copy(me, send_dn, dn_dev, own_ref).start())
    pl.when(z < LAYERS - 1)(lambda: row_copy(me, send_up, up_dev, own_ref).start())
    row_copy(me, send_core, core_dev, own_ref).start()
    rows[span(me), :] = own_ref[...]

    def from_line(layer, sems, onward, dev):
        b = block(layer, x, c)
        arrived(b)
        pl.when(onward)(lambda: row_copy(b, sems, dev).start())
        row_copy(b, send_x, x_dev).start()
        row_copy(b, send_core, core_dev).start()

    def line_step(s):
        pl.when(z >= s)(lambda: from_line(z - s, send_up, z < LAYERS - 1, up_dev))
        pl.when(z + s < LAYERS)(lambda: from_line(z + s, send_dn, z > 0, dn_dev))

    def rest_of(layer):
        b = block(layer, 1 - x, c)
        arrived(b)
        row_copy(b, send_core, core_dev).start()
        arrived(block(layer, 0, 1 - c))
        arrived(block(layer, 1, 1 - c))

    def layer_span(layer):
        return pl.ds(pl.multiple_of(layer * 4 * n, 4 * n), 4 * n)

    def compute(layer, first):
        if first:
            loads[0].wait()
            loads[1].wait()
        where = layer_span(layer)

        @pl.loop(0, inner // 256)
        def _(i):
            cols = pl.ds(pl.multiple_of(i * 256, 256), 256)
            inputs = rows[where, :width]
            g = jnp.dot(inputs, gate[:, cols], preferred_element_type=jnp.float32)
            u = jnp.dot(inputs, up[:, cols], preferred_element_type=jnp.float32)
            hidden[:, cols] = (g / (1.0 + jnp.exp(-g)) * u).astype(jnp.bfloat16)

        if first:
            loads[2].wait()
        lane = lax.broadcasted_iota(jnp.int32, (4 * n, full - width), 1)
        mine = (lane == me) | (lane == me + experts) | (lane == me + 2 * experts)
        factor = jnp.sum(
            jnp.where(mine, rows[where, width:].astype(jnp.float32), 0.0), axis=1, keepdims=True
        )

        @pl.loop(0, width // 512)
        def _(i):
            cols = pl.ds(pl.multiple_of(i * 512, 512), 512)
            o = jnp.dot(hidden[...], down[:, cols], preferred_element_type=jnp.float32)
            parts[where, cols] = (o * factor).astype(jnp.bfloat16)

        for xx in range(2):
            core_back(layer, xx, 1 - c).start()

    def core_back(layer, xx, cc):
        slot = layer * 2 + xx
        return remote(
            parts.at[span(block(layer, xx, cc))], from_core.at[slot],
            back_core.at[slot], got_core.at[slot], core_dev,
        )

    def x_back(layer):
        return remote(
            parts.at[span(block(layer, 1 - x, c))], from_x.at[layer],
            back_x.at[layer], got_x.at[layer], x_dev,
        )

    def z_back(layer, slot, dev):
        return remote(
            parts.at[span(block(layer, x, c))], from_z.at[slot],
            back_z.at[layer], got_z.at[slot], dev,
        )

    def add_up(dst, dst_rows, terms):
        @pl.loop(0, width // 512)
        def _(i):
            cols = pl.ds(pl.multiple_of(i * 512, 512), 512)
            total = None
            for ref, where in terms:
                term = ref[where, cols].astype(jnp.float32)
                total = term if total is None else total + term
            dst[dst_rows, cols] = total.astype(jnp.bfloat16)

    whole = slice(None)

    def ret_x(layer):
        core_back(layer, 1 - x, c).wait_recv()
        b = span(block(layer, 1 - x, c))
        add_up(parts, b, [(parts, b), (from_core.at[layer * 2 + 1 - x], whole)])
        x_back(layer).start()

    def ret_z(layer):
        core_back(layer, x, c).wait_recv()
        x_back(layer).wait_recv()
        b = span(block(layer, x, c))
        terms = [
            (parts, b), (from_core.at[layer * 2 + x], whole), (from_x.at[layer], whole),
        ]
        carries = ((layer > z) & (z > 0)) | ((layer < z) & (z < LAYERS - 1))

        @pl.when(carries)
        def _():
            z_back(layer, layer, up_dev).wait_recv()
            add_up(parts, b, terms + [(from_z.at[layer], whole)])

        @pl.when(jnp.logical_not(carries))
        def _():
            add_up(parts, b, terms)

        @pl.when(layer > z)
        def _():
            z_back(layer, layer, up_dev).start()

        @pl.when((layer < z) & (layer < z - 1))
        def _():
            z_back(layer, layer, dn_dev).start()

        @pl.when((layer < z) & (layer == z - 1))
        def _():
            z_back(layer, LAYERS, dn_dev).start()

    order = [
        z,
        pick((1, 2, 1, 2), z),
        pick((2, 0, 3, 1), z),
        pick((3, 3, 0, 0), z),
    ]
    back_order = [order[1], pick((2, 3, 0, 1), z), pick((3, 0, 3, 0), z)]

    line_step(1)
    rest_of(order[0])
    compute(order[0], True)
    line_step(2)
    rest_of(order[1])
    compute(order[1], False)
    ret_x(order[0])
    line_step(3)
    rest_of(order[2])
    compute(order[2], False)
    ret_x(order[1])
    rest_of(order[3])
    compute(order[3], False)
    ret_x(order[2])
    ret_x(order[3])
    for layer in back_order:
        ret_z(layer)

    core_back(z, x, c).wait_recv()
    x_back(z).wait_recv()
    b = span(me)
    terms = [
        (stream_ref, whole), (parts, b), (from_core.at[z * 2 + x], whole), (from_x.at[z], whole),
    ]
    below, above = (from_z.at[z], whole), (from_z.at[LAYERS], whole)

    @pl.when(z > 0)
    def _():
        z_back(z, z, up_dev).wait_recv()

    @pl.when(z < LAYERS - 1)
    def _():
        z_back(z, LAYERS, up_dev).wait_recv()

    @pl.when(z == 0)
    def _():
        add_up(out_ref, whole, terms + [above])

    @pl.when(z == LAYERS - 1)
    def _():
        add_up(out_ref, whole, terms + [below])

    @pl.when((z > 0) & (z < LAYERS - 1))
    def _():
        add_up(out_ref, whole, terms + [below, above])

    for layer in range(LAYERS):
        mine = block(layer, x, c)
        row_copy(mine, send_x, x_dev).wait_send()
        row_copy(mine, send_core, core_dev).wait_send()
        row_copy(block(layer, 1 - x, c), send_core, core_dev).wait_send()

        @pl.when((layer <= z) & (z < LAYERS - 1))
        def _():
            row_copy(mine, send_up, up_dev).wait_send()

        @pl.when((layer >= z) & (z > 0))
        def _():
            row_copy(mine, send_dn, dn_dev).wait_send()

        for xx in range(2):
            core_back(layer, xx, 1 - c).wait_send()
        x_back(layer).wait_send()

        @pl.when(z != layer)
        def _():
            z_back(layer, layer, up_dev).wait_send()


def expert_layer(own, stream, gate, up, down):
    n, width = stream.shape
    full = own.shape[1]
    inner = gate.shape[2]
    total = 4 * LAYERS
    dma = pltpu.SemaphoreType.DMA
    bf16 = jnp.bfloat16
    return pl.pallas_call(
        layer_kernel,
        out_shape=jax.ShapeDtypeStruct((n, width), bf16),
        in_specs=[pl.BlockSpec(memory_space=pltpu.VMEM)] * 2
        + [pl.BlockSpec(memory_space=pl.ANY)] * 3,
        out_specs=pl.BlockSpec(memory_space=pltpu.VMEM),
        scratch_shapes=[
            pltpu.VMEM((total * n, full), bf16),
            pltpu.VMEM((total * n, width), bf16),
            pltpu.VMEM((2 * LAYERS, n, width), bf16),
            pltpu.VMEM((LAYERS, n, width), bf16),
            pltpu.VMEM((LAYERS + 1, n, width), bf16),
            pltpu.VMEM((4 * n, inner), bf16),
            pltpu.VMEM((width, inner), bf16),
            pltpu.VMEM((width, inner), bf16),
            pltpu.VMEM((inner, width), bf16),
            dma((total,)), dma((total,)), dma((total,)), dma((total,)), dma((total,)),
            dma((2 * LAYERS,)), dma((LAYERS,)), dma((LAYERS,)),
            dma((2 * LAYERS,)), dma((LAYERS,)), dma((LAYERS + 1,)),
            dma((3,)),
        ],
        compiler_params=pltpu.CompilerParams(
            collective_id=0, has_side_effects=True, vmem_limit_bytes=60 * 1024 * 1024
        ),
    )(own, stream, gate, up, down)


def dense(
    residual, head_partials, norm_gain, router_weight, routes, expert_gate, expert_up, expert_down
):
    expert_count = router_weight.shape[1]
    stream, normed = prepare(residual, head_partials[0].astype(jnp.float32), norm_gain)
    payload, scales = quantize(normed, QBLOCK)
    weights = route_weights(normed, router_weight, routes)
    spread = split_three(spread_weights(weights, routes, expert_count))
    spread = jnp.pad(spread, ((0, 0), (0, 128 - spread.shape[1])))
    own = jnp.concatenate([dequantize(payload, scales), spread], axis=1)
    return expert_layer(own, stream, expert_gate, expert_up, expert_down)


def local(*args):
    if lax.axis_size("tensor") == 1 and lax.axis_size("expert") == 4 * LAYERS:
        return dense(*args)
    return routed(*args)


def solution(mesh):
    return jax.shard_map(
        local,
        mesh=mesh,
        in_specs=(
            P(("group", "expert", "tensor"), None),
            P("tensor", ("group", "expert"), None),
            P(),
            P(),
            P(("group", "expert", "tensor"), None),
            P("expert", None, "tensor"),
            P("expert", None, "tensor"),
            P("expert", "tensor", None),
        ),
        out_specs=P(("group", "expert", "tensor"), None),
        check_vma=False,
    )
```

profile of v0, /device:TPU:0, one launch (start us, length us, event | category | flops | bytes accessed | tf_op | source)
XLA Modules:
  0.0 139.9 jit_solution(7088785935190949771)
XLA Ops:
  0.0 0.0 copy-start
  0.0 0.0 copy-start.2
  0.0 1.5 %fusion.3 = (f32[64]{0:T(128)S(1)}, bf16[64,3584]{1,0:T(8,128)(2,1)S(1)}) fusion(bf16[1,64,3584]{2,1,0:T(8,128)(2,1)} %param.9, bf16[64,3584]{1,0:T(8,128)(2,1)} %param.8), kind=kLoop, calls=%fused_computation.6 | loop fusion | flops 1605568 | bytes 1376512 | tf_op jit(solution)/shard_map/reduce_sum | solution.py:20
  1.5 0.0 copy-start.1
  1.5 0.0 copy-done
  1.5 1.7 %fusion.2 = f32[64,16]{0,1:T(8,128)S(1)} fusion(f32[3584,16]{0,1:T(8,128)S(1)} %copy-done, bf16[64,3584]{1,0:T(8,128)(2,1)S(1)} %get-tuple-element.8.stream_ref, f32[3584]{0:T(1024)} %param.10, f32[64]{0:T(128)S(1)} %add_rsqrt_fusion), kind=kOutput, calls=%fused_computation.5 | convolution fusion | flops 44731392 | bytes 706816 | tf_op jit(solution)/shard_map/dot_general | solution.py:42
  3.2 0.7 select_reduce_fusion
  4.0 0.7 select_reduce_fusion.2
  4.7 0.1 copy.16
  4.8 0.1 copy.15
  4.9 0.1 fusion.19
  5.0 0.9 fusion.7
  5.9 0.2 abs.7
  6.1 0.3 reduce_max.9
  6.4 0.3 div.42
  6.8 0.0 copy-done.2
  6.8 0.7 fusion.9
  7.5 0.8 pad_maximum_fusion.own_ref
  8.3 0.0 copy-done.1
  8.3 129.8 %shard_map.82 = bf16[64,3584]{1,0:T(8,128)(2,1)} custom-call(bf16[64,3712]{1,0:T(8,128)(2,1)} %pad_maximum_fusion.own_ref, bf16[64,3584]{1,0:T(8,128)(2,1)} %copy-done.1, bf16[1,3584,1024]{2,1,0:T(8,128)(2,1)} %gate_hbm.1, bf16[1,3584,1024]{2,1,0:T(8,128)(2,1)} %up_hbm.1, bf16[1,1024,3584]{2,1,0:T(8,128)(2,1)} %down_hbm.1), custom_call_target="tpu_custom_call" | custom-call | tf_op jit(solution)/shard_map/pallas_call | solution.py:415
  138.1 1.8 %copy.24 = bf16[64,3584]{1,0:T(8,128)(2,1)} copy(bf16[64,3584]{1,0:T(8,128)(2,1)} %shard_map.82) | data formatting | bytes 917504
  (5 shorter events, 0.0 us)
Async XLA Ops:
  0.0 1.5 %copy-start = (f32[3584,16]{0,1:T(8,128)S(1)}, f32[3584,16]{0,1:T(8,128)}, u32[]{:S(2)}) copy-start(f32[3584,16]{0,1:T(8,128)} %param.11) | copy-start | bytes 688132
  0.0 6.8 %copy-start.2 = (f32[3584]{0:T(1024)S(1)}, f32[3584]{0:T(1024)}, u32[]{:S(2)}) copy-start(f32[3584]{0:T(1024)} %param.10) | copy-start | bytes 43012
  1.5 6.8 %copy-start.1 = (bf16[64,3584]{1,0:T(8,128)(2,1)}, bf16[64,3584]{1,0:T(8,128)(2,1)S(1)}, u32[]{:S(2)}) copy-start(bf16[64,3584]{1,0:T(8,128)(2,1)S(1)} %get-tuple-element.8.stream_ref) | copy-start | bytes 1376260
where the time goes:
time: 140 us
  Pallas kernels  130 us (93%)
  other arithmetic  5.78 us (4%)
  local copies, waits for them, and re-layouts  2.52 us (2%)
  matrix products  1.71 us (1%)
    pallas_call x1, Pallas kernels, expert_layer(): pl.pallas_call(layer_kernel, out_shape=jax.ShapeDtypeStruct((n, width), b...  130 us

commit v1 on v0

--- a/solution.py
+++ b/solution.py
@@ -230,10 +230,13 @@
     def layer_span(layer):
         return pl.ds(pl.multiple_of(layer * 4 * n, 4 * n), 4 * n)
 
-    def compute(layer, first):
-        if first:
-            loads[0].wait()
-            loads[1].wait()
+    half = (width // 512 + 1) // 2 * 512
+    chunks = ((0, half), (half, width - half))
+
+    def part(h):
+        return pl.ds(chunks[h][0], chunks[h][1])
+
+    def gate_up(layer):
         where = layer_span(layer)
 
         @pl.loop(0, inner // 256)
@@ -244,44 +247,45 @@
             u = jnp.dot(inputs, up[:, cols], preferred_element_type=jnp.float32)
             hidden[:, cols] = (g / (1.0 + jnp.exp(-g)) * u).astype(jnp.bfloat16)
 
-        if first:
-            loads[2].wait()
+    def down_back(layer):
+        where = layer_span(layer)
         lane = lax.broadcasted_iota(jnp.int32, (4 * n, full - width), 1)
         mine = (lane == me) | (lane == me + experts) | (lane == me + 2 * experts)
         factor = jnp.sum(
             jnp.where(mine, rows[where, width:].astype(jnp.float32), 0.0), axis=1, keepdims=True
         )
-
-        @pl.loop(0, width // 512)
-        def _(i):
-            cols = pl.ds(pl.multiple_of(i * 512, 512), 512)
-            o = jnp.dot(hidden[...], down[:, cols], preferred_element_type=jnp.float32)
-            parts[where, cols] = (o * factor).astype(jnp.bfloat16)
-
-        for xx in range(2):
-            core_back(layer, xx, 1 - c).start()
-
-    def core_back(layer, xx, cc):
+        for h in range(2):
+
+            @pl.loop(chunks[h][0] // 512, sum(chunks[h]) // 512)
+            def _(i):
+                cols = pl.ds(pl.multiple_of(i * 512, 512), 512)
+                o = jnp.dot(hidden[...], down[:, cols], preferred_element_type=jnp.float32)
+                parts[where, cols] = (o * factor).astype(jnp.bfloat16)
+
+            for xx in (1 - x, x):
+                core_back(layer, xx, 1 - c, h).start()
+
+    def core_back(layer, xx, cc, h):
         slot = layer * 2 + xx
         return remote(
-            parts.at[span(block(layer, xx, cc))], from_core.at[slot],
-            back_core.at[slot], got_core.at[slot], core_dev,
-        )
-
-    def x_back(layer):
+            parts.at[span(block(layer, xx, cc)), part(h)], from_core.at[slot, :, part(h)],
+            back_core.at[slot, h], got_core.at[slot, h], core_dev,
+        )
+
+    def x_back(layer, h):
         return remote(
-            parts.at[span(block(layer, 1 - x, c))], from_x.at[layer],
-            back_x.at[layer], got_x.at[layer], x_dev,
-        )
-
-    def z_back(layer, slot, dev):
+            parts.at[span(block(layer, 1 - x, c)), part(h)], from_x.at[layer, :, part(h)],
+            back_x.at[layer, h], got_x.at[layer, h], x_dev,
+        )
+
+    def z_back(layer, slot, dev, h):
         return remote(
-            parts.at[span(block(layer, x, c))], from_z.at[slot],
-            back_z.at[layer], got_z.at[slot], dev,
-        )
-
-    def add_up(dst, dst_rows, terms):
-        @pl.loop(0, width // 512)
+            parts.at[span(block(layer, x, c)), part(h)], from_z.at[slot, :, part(h)],
+            back_z.at[layer, h], got_z.at[slot, h], dev,
+        )
+
+    def add_up(dst, dst_rows, terms, h):
+        @pl.loop(chunks[h][0] // 512, sum(chunks[h]) // 512)
         def _(i):
             cols = pl.ds(pl.multiple_of(i * 512, 512), 512)
             total = None
@@ -293,40 +297,42 @@
     whole = slice(None)
 
     def ret_x(layer):
-        core_back(layer, 1 - x, c).wait_recv()
         b = span(block(layer, 1 - x, c))
-        add_up(parts, b, [(parts, b), (from_core.at[layer * 2 + 1 - x], whole)])
-        x_back(layer).start()
+        for h in range(2):
+            core_back(layer, 1 - x, c, h).wait_recv()
+            add_up(parts, b, [(parts, b), (from_core.at[layer * 2 + 1 - x], whole)], h)
+            x_back(layer, h).start()
 
     def ret_z(layer):
-        core_back(layer, x, c).wait_recv()
-        x_back(layer).wait_recv()
         b = span(block(layer, x, c))
         terms = [
             (parts, b), (from_core.at[layer * 2 + x], whole), (from_x.at[layer], whole),
         ]
         carries = ((layer > z) & (z > 0)) | ((layer < z) & (z < LAYERS - 1))
-
-        @pl.when(carries)
-        def _():
-            z_back(layer, layer, up_dev).wait_recv()
-            add_up(parts, b, terms + [(from_z.at[layer], whole)])
-
-        @pl.when(jnp.logical_not(carries))
-        def _():
-            add_up(parts, b, terms)
-
-        @pl.when(layer > z)
-        def _():
-            z_back(layer, layer, up_dev).start()
-
-        @pl.when((layer < z) & (layer < z - 1))
-        def _():
-            z_back(layer, layer, dn_dev).start()
-
-        @pl.when((layer < z) & (layer == z - 1))
-        def _():
-            z_back(layer, LAYERS, dn_dev).start()
+        for h in range(2):
+            core_back(layer, x, c, h).wait_recv()
+            x_back(layer, h).wait_recv()
+
+            @pl.when(carries)
+            def _():
+                z_back(layer, layer, up_dev, h).wait_recv()
+                add_up(parts, b, terms + [(from_z.at[layer], whole)], h)
+
+            @pl.when(jnp.logical_not(carries))
+            def _():
+                add_up(parts, b, terms, h)
+
+            @pl.when(layer > z)
+            def _():
+                z_back(layer, layer, up_dev, h).start()
+
+            @pl.when((layer < z) & (layer < z - 1))
+            def _():
+                z_back(layer, layer, dn_dev, h).start()
+
+            @pl.when((layer < z) & (layer == z - 1))
+            def _():
+                z_back(layer, LAYERS, dn_dev, h).start()
 
     order = [
         z,
@@ -335,52 +341,67 @@
         pick((3, 3, 0, 0), z),
     ]
     back_order = [order[1], pick((2, 3, 0, 1), z), pick((3, 0, 3, 0), z)]
+    ends = (z == 0) | (z == LAYERS - 1)
 
     line_step(1)
     rest_of(order[0])
-    compute(order[0], True)
+    loads[0].wait()
+    loads[1].wait()
+    gate_up(order[0])
+    loads[2].wait()
+    down_back(order[0])
     line_step(2)
     rest_of(order[1])
-    compute(order[1], False)
-    ret_x(order[0])
+    gate_up(order[1])
+    down_back(order[1])
     line_step(3)
     rest_of(order[2])
-    compute(order[2], False)
+    gate_up(order[2])
     ret_x(order[1])
+    down_back(order[2])
     rest_of(order[3])
-    compute(order[3], False)
+    gate_up(order[3])
     ret_x(order[2])
+    pl.when(ends)(lambda: ret_z(order[1]))
+    down_back(order[3])
     ret_x(order[3])
-    for layer in back_order:
-        ret_z(layer)
-
-    core_back(z, x, c).wait_recv()
-    x_back(z).wait_recv()
+    pl.when(ends)(lambda: ret_z(order[2]))
+    ret_x(order[0])
+    pl.when(ends)(lambda: ret_z(order[3]))
+
+    @pl.when(jnp.logical_not(ends))
+    def _():
+        for layer in back_order:
+            ret_z(layer)
+
     b = span(me)
     terms = [
         (stream_ref, whole), (parts, b), (from_core.at[z * 2 + x], whole), (from_x.at[z], whole),
     ]
     below, above = (from_z.at[z], whole), (from_z.at[LAYERS], whole)
-
-    @pl.when(z > 0)
-    def _():
-        z_back(z, z, up_dev).wait_recv()
-
-    @pl.when(z < LAYERS - 1)
-    def _():
-        z_back(z, LAYERS, up_dev).wait_recv()
-
-    @pl.when(z == 0)
-    def _():
-        add_up(out_ref, whole, terms + [above])
-
-    @pl.when(z == LAYERS - 1)
-    def _():
-        add_up(out_ref, whole, terms + [below])
-
-    @pl.when((z > 0) & (z < LAYERS - 1))
-    def _():
-        add_up(out_ref, whole, terms + [below, above])
+    for h in range(2):
+        core_back(z, x, c, h).wait_recv()
+        x_back(z, h).wait_recv()
+
+        @pl.when(z > 0)
+        def _():
+            z_back(z, z, up_dev, h).wait_recv()
+
+        @pl.when(z < LAYERS - 1)
+        def _():
+            z_back(z, LAYERS, up_dev, h).wait_recv()
+
+        @pl.when(z == 0)
+        def _():
+            add_up(out_ref, whole, terms + [above], h)
+
+        @pl.when(z == LAYERS - 1)
+        def _():
+            add_up(out_ref, whole, terms + [below], h)
+
+        @pl.when((z > 0) & (z < LAYERS - 1))
+        def _():
+            add_up(out_ref, whole, terms + [below, above], h)
 
     for layer in range(LAYERS):
         mine = block(layer, x, c)
@@ -396,13 +417,14 @@
         def _():
             row_copy(mine, send_dn, dn_dev).wait_send()
 
-        for xx in range(2):
-            core_back(layer, xx, 1 - c).wait_send()
-        x_back(layer).wait_send()
-
-        @pl.when(z != layer)
-        def _():
-            z_back(layer, layer, up_dev).wait_send()
+        for h in range(2):
+            for xx in range(2):
+                core_back(layer, xx, 1 - c, h).wait_send()
+            x_back(layer, h).wait_send()
+
+            @pl.when(z != layer)
+            def _():
+                z_back(layer, layer, up_dev, h).wait_send()
 
 
 def expert_layer(own, stream, gate, up, down):
@@ -429,8 +451,8 @@
             pltpu.VMEM((width, inner), bf16),
             pltpu.VMEM((inner, width), bf16),
             dma((total,)), dma((total,)), dma((total,)), dma((total,)), dma((total,)),
-            dma((2 * LAYERS,)), dma((LAYERS,)), dma((LAYERS,)),
-            dma((2 * LAYERS,)), dma((LAYERS,)), dma((LAYERS + 1,)),
+            dma((2 * LAYERS, 2)), dma((LAYERS, 2)), dma((LAYERS, 2)),
+            dma((2 * LAYERS, 2)), dma((LAYERS, 2)), dma((LAYERS + 1, 2)),
             dma((3,)),
         ],
         compiler_params=pltpu.CompilerParams(

time: 140 us -> 118 us (0.84)
  Pallas kernels: 130 us -> 108 us
    pallas_call x1, Pallas kernels: 130 us -> 108 us  [expert_layer(): pl.pallas_call(layer_kernel, out_shape=jax.ShapeDtypeStruct((n, width), b...]
where the time goes in v1:
time: 118 us
  Pallas kernels  108 us (92%)
  other arithmetic  5.78 us (5%)
  local copies, waits for them, and re-layouts  2.52 us (2%)
  matrix products  1.71 us (1%)
    pallas_call x1, Pallas kernels, expert_layer(): pl.pallas_call(layer_kernel, out_shape=jax.ShapeDtypeStruct((n, width), b...  108 us

profile of v1, /device:TPU:0, one launch (start us, length us, event | category | flops | bytes accessed | tf_op | source)
XLA Modules:
  0.0 117.8 jit_solution(17275114332915830013)
XLA Ops:
  0.0 0.0 copy-start
  0.0 0.0 copy-start.2
  0.0 1.5 %fusion.3 = (f32[64]{0:T(128)S(1)}, bf16[64,3584]{1,0:T(8,128)(2,1)S(1)}) fusion(bf16[1,64,3584]{2,1,0:T(8,128)(2,1)} %param.9, bf16[64,3584]{1,0:T(8,128)(2,1)} %param.8), kind=kLoop, calls=%fused_computation.6 | loop fusion | flops 1605568 | bytes 1376512 | tf_op jit(solution)/shard_map/reduce_sum | solution.py:20
  1.5 0.0 copy-start.1
  1.5 0.0 copy-done
  1.5 1.7 %fusion.2 = f32[64,16]{0,1:T(8,128)S(1)} fusion(f32[3584,16]{0,1:T(8,128)S(1)} %copy-done, bf16[64,3584]{1,0:T(8,128)(2,1)S(1)} %get-tuple-element.8.stream_ref, f32[3584]{0:T(1024)} %param.10, f32[64]{0:T(128)S(1)} %add_rsqrt_fusion), kind=kOutput, calls=%fused_computation.5 | convolution fusion | flops 44731392 | bytes 706816 | tf_op jit(solution)/shard_map/dot_general | solution.py:42
  3.2 0.7 select_reduce_fusion
  4.0 0.7 select_reduce_fusion.2
  4.7 0.1 copy.16
  4.8 0.1 copy.15
  4.9 0.1 fusion.19
  5.0 0.9 fusion.7
  5.9 0.2 abs.7
  6.1 0.3 reduce_max.9
  6.4 0.3 div.42
  6.8 0.0 copy-done.2
  6.8 0.7 fusion.9
  7.5 0.8 pad_maximum_fusion.own_ref
  8.3 0.0 copy-done.1
  8.3 107.7 %shard_map.82 = bf16[64,3584]{1,0:T(8,128)(2,1)} custom-call(bf16[64,3712]{1,0:T(8,128)(2,1)} %pad_maximum_fusion.own_ref, bf16[64,3584]{1,0:T(8,128)(2,1)} %copy-done.1, bf16[1,3584,1024]{2,1,0:T(8,128)(2,1)} %gate_hbm.1, bf16[1,3584,1024]{2,1,0:T(8,128)(2,1)} %up_hbm.1, bf16[1,1024,3584]{2,1,0:T(8,128)(2,1)} %down_hbm.1), custom_call_target="tpu_custom_call" | custom-call | tf_op jit(solution)/shard_map/pallas_call | solution.py:437
  116.0 1.8 %copy.24 = bf16[64,3584]{1,0:T(8,128)(2,1)} copy(bf16[64,3584]{1,0:T(8,128)(2,1)} %shard_map.82) | data formatting | bytes 917504
  (5 shorter events, 0.0 us)
Async XLA Ops:
  0.0 1.5 %copy-start = (f32[3584,16]{0,1:T(8,128)S(1)}, f32[3584,16]{0,1:T(8,128)}, u32[]{:S(2)}) copy-start(f32[3584,16]{0,1:T(8,128)} %param.11) | copy-start | bytes 688132
  0.0 6.8 %copy-start.2 = (f32[3584]{0:T(1024)S(1)}, f32[3584]{0:T(1024)}, u32[]{:S(2)}) copy-start(f32[3584]{0:T(1024)} %param.10) | copy-start | bytes 43012
  1.5 6.8 %copy-start.1 = (bf16[64,3584]{1,0:T(8,128)(2,1)}, bf16[64,3584]{1,0:T(8,128)(2,1)S(1)}, u32[]{:S(2)}) copy-start(bf16[64,3584]{1,0:T(8,128)(2,1)S(1)} %get-tuple-element.8.stream_ref) | copy-start | bytes 1376260

commit v2 on v1

--- a/solution.py
+++ b/solution.py
@@ -132,28 +132,69 @@
     return value
 
 
-def spread_weights(weights, routes, expert_count):
-    labels = jnp.arange(expert_count, dtype=jnp.int32)
-    return jnp.sum(
-        jnp.where(routes[:, :, None] == labels[None, None, :], weights[:, :, None], 0.0), axis=1
-    )
-
-
-def split_three(value):
-    first = lax.reduce_precision(value, 8, 7)
-    second = lax.reduce_precision(value - first, 8, 7)
-    third = value - first - second
-    return jnp.concatenate([first, second, third], axis=1).astype(jnp.bfloat16)
+def local_rows(
+    residual_ref, heads_ref, gain_ref, router_ref, routes_ref,
+    stream_ref, normed_ref, spread_ref, rows, mine,
+):
+    n, width = residual_ref.shape
+    experts = router_ref.shape[0]
+    top_count = routes_ref.shape[1]
+
+    def block_cols(i):
+        return pl.ds(pl.multiple_of(i * QBLOCK, QBLOCK), QBLOCK)
+
+    def add_attention(i, squares):
+        cols = block_cols(i)
+        value = residual_ref[:, cols].astype(jnp.float32) + heads_ref[:, cols].astype(jnp.float32)
+        value = value.astype(jnp.bfloat16)
+        stream_ref[:, cols] = value
+        value = value.astype(jnp.float32)
+        return squares + value * value
+
+    squares = lax.fori_loop(
+        0, width // QBLOCK, add_attention, jnp.zeros((n, QBLOCK), jnp.float32), unroll=4
+    )
+    factor = lax.rsqrt(jnp.sum(squares, axis=1, keepdims=True) * (1.0 / width) + epsilon)
+
+    def scale_block(i, carry):
+        cols = block_cols(i)
+        normed = stream_ref[:, cols].astype(jnp.float32) * factor * gain_ref[:, cols]
+        normed_ref[:, cols] = normed
+        scale = (jnp.max(jnp.abs(normed), axis=1, keepdims=True) + epsilon) / scale_limit
+        scale = scale.astype(jnp.bfloat16).astype(jnp.float32)
+        payload = (normed / scale).astype(jnp.bfloat16).astype(jnp.float32)
+        rows[mine, cols] = (payload * scale).astype(jnp.bfloat16)
+        return carry
+
+    lax.fori_loop(0, width // QBLOCK, scale_block, 0, unroll=4)
+
+    logits = lax.dot_general(
+        normed_ref[...], router_ref[...], (((1,), (1,)), ((), ())),
+        precision=lax.Precision.HIGHEST, preferred_element_type=jnp.float32,
+    )
+    affinity = 1.0 / (1.0 + jnp.exp(-logits))
+    labels = lax.broadcasted_iota(jnp.int32, (n, experts), 1)
+    picked = jnp.zeros((n, experts), jnp.float32)
+    for k in range(top_count):
+        picked = picked + jnp.where(routes_ref[:, k : k + 1] == labels, affinity, 0.0)
+    weights = route_scale * picked / jnp.sum(picked, axis=1, keepdims=True)
+    spread_ref[...] = jnp.zeros_like(spread_ref)
+    for piece in range(3):
+        top = weights.astype(jnp.bfloat16).astype(jnp.float32)
+        spread_ref[:, piece * experts : (piece + 1) * experts] = top
+        weights = weights - top
+    rows[mine, width:] = spread_ref[...].astype(jnp.bfloat16)
 
 
 def layer_kernel(
-    own_ref, stream_ref, gate_hbm, up_hbm, down_hbm, out_ref,
+    residual_ref, heads_ref, gain_ref, router_ref, routes_ref, gate_hbm, up_hbm, down_hbm, out_ref,
+    stream_ref, normed_ref, spread_ref,
     rows, parts, from_core, from_x, from_z, hidden, gate, up, down,
     send_up, send_dn, send_x, send_core, got_rows,
     back_core, back_x, back_z, got_core, got_x, got_z, weight_sem,
 ):
     n, width = stream_ref.shape
-    full = own_ref.shape[1]
+    full = rows.shape[1]
     inner = hidden.shape[1]
     experts = LAYERS * 4
     me = lax.axis_index("expert")
@@ -186,6 +227,10 @@
     ]
     for load in loads:
         load.start()
+    local_rows(
+        residual_ref, heads_ref, gain_ref, router_ref, routes_ref,
+        stream_ref, normed_ref, spread_ref, rows, span(me),
+    )
     pl.semaphore_wait(barrier, 2 + (z + LAYERS - 1) // LAYERS + (2 * LAYERS - 2 - z) // LAYERS)
 
     def remote(src, dst, ssem, rsem, dev):
@@ -194,20 +239,16 @@
             device_id={"expert": dev}, device_id_type=pl.DeviceIdType.MESH,
         )
 
-    def row_copy(b, sems, dev, src=None):
-        return remote(
-            rows.at[span(b)] if src is None else src,
-            rows.at[span(b)], sems.at[b], got_rows.at[b], dev,
-        )
+    def row_copy(b, sems, dev):
+        return remote(rows.at[span(b)], rows.at[span(b)], sems.at[b], got_rows.at[b], dev)
 
     def arrived(b):
         row_copy(b, send_core, core_dev).wait_recv()
 
-    row_copy(me, send_x, x_dev, own_ref).start()
-    pl.when(z > 0)(lambda: row_copy(me, send_dn, dn_dev, own_ref).start())
-    pl.when(z < LAYERS - 1)(lambda: row_copy(me, send_up, up_dev, own_ref).start())
-    row_copy(me, send_core, core_dev, own_ref).start()
-    rows[span(me), :] = own_ref[...]
+    row_copy(me, send_x, x_dev).start()
+    pl.when(z > 0)(lambda: row_copy(me, send_dn, dn_dev).start())
+    pl.when(z < LAYERS - 1)(lambda: row_copy(me, send_up, up_dev).start())
+    row_copy(me, send_core, core_dev).start()
 
     def from_line(layer, sems, onward, dev):
         b = block(layer, x, c)
@@ -427,20 +468,25 @@
                 z_back(layer, layer, up_dev, h).wait_send()
 
 
-def expert_layer(own, stream, gate, up, down):
-    n, width = stream.shape
-    full = own.shape[1]
-    inner = gate.shape[2]
+def dense(
+    residual, head_partials, norm_gain, router_weight, routes, expert_gate, expert_up, expert_down
+):
+    n, width = residual.shape
+    full = width + 128
+    inner = expert_gate.shape[2]
     total = 4 * LAYERS
     dma = pltpu.SemaphoreType.DMA
     bf16 = jnp.bfloat16
     return pl.pallas_call(
         layer_kernel,
         out_shape=jax.ShapeDtypeStruct((n, width), bf16),
-        in_specs=[pl.BlockSpec(memory_space=pltpu.VMEM)] * 2
+        in_specs=[pl.BlockSpec(memory_space=pltpu.VMEM)] * 5
         + [pl.BlockSpec(memory_space=pl.ANY)] * 3,
         out_specs=pl.BlockSpec(memory_space=pltpu.VMEM),
         scratch_shapes=[
+            pltpu.VMEM((n, width), bf16),
+            pltpu.VMEM((n, width), jnp.float32),
+            pltpu.VMEM((n, 128), jnp.float32),
             pltpu.VMEM((total * n, full), bf16),
             pltpu.VMEM((total * n, width), bf16),
             pltpu.VMEM((2 * LAYERS, n, width), bf16),
@@ -458,20 +504,10 @@
         compiler_params=pltpu.CompilerParams(
             collective_id=0, has_side_effects=True, vmem_limit_bytes=60 * 1024 * 1024
         ),
-    )(own, stream, gate, up, down)
-
-
-def dense(
-    residual, head_partials, norm_gain, router_weight, routes, expert_gate, expert_up, expert_down
-):
-    expert_count = router_weight.shape[1]
-    stream, normed = prepare(residual, head_partials[0].astype(jnp.float32), norm_gain)
-    payload, scales = quantize(normed, QBLOCK)
-    weights = route_weights(normed, router_weight, routes)
-    spread = split_three(spread_weights(weights, routes, expert_count))
-    spread = jnp.pad(spread, ((0, 0), (0, 128 - spread.shape[1])))
-    own = jnp.concatenate([dequantize(payload, scales), spread], axis=1)
-    return expert_layer(own, stream, expert_gate, expert_up, expert_down)
+    )(
+        residual, head_partials[0], norm_gain[None], router_weight.T, routes,
+        expert_gate, expert_up, expert_down,
+    )
 
 
 def local(*args):

time: 118 us -> 114 us (0.966)
  other arithmetic: 5.78 us -> 0 us
  local copies, waits for them, and re-layouts: 2.52 us -> 4.52 us
  matrix products: 1.71 us -> 0 us
    reduce_sum x3 -> x0, other arithmetic: 2.9 us -> none  [the longest x1 1.46 us: prepare(): jnp.mean(values * values, axis=-1, keepdims=True) + epsilon]
    dot_general x1 -> x0, matrix products: 1.71 us -> none  [route_weights(): jnp.dot(normed, router_weight, precision=lax.Precision.HIGHEST, preferred...]
    unnamed x7 -> x2, local copies, waits for them, and re-layouts: 1.83 us -> 3.2 us
    pallas_call x1, Pallas kernels: 108 us -> 109 us  [dense(): pl.pallas_call(layer_kernel, out_shape=jax.ShapeDtypeStruct((n, width), b...]
    broadcast_in_dim x0 -> x1, local copies, waits for them, and re-layouts: none -> 1.32 us  [dense(): norm_gain[None]]
where the time goes in v2:
time: 114 us
  Pallas kernels  109 us (96%)
  local copies, waits for them, and re-layouts  4.52 us (4%)
    pallas_call x1, Pallas kernels, dense(): pl.pallas_call(layer_kernel, out_shape=jax.ShapeDtypeStruct((n, width), b...  109 us
    unnamed x2, local copies, waits for them, and re-layouts  3.2 us

profile of v2, /device:TPU:0, one launch (start us, length us, event | category | flops | bytes accessed | tf_op | source)
XLA Modules:
  0.0 113.5 jit_solution(8619149867807146076)
XLA Ops:
  0.0 1.3 %broadcast_in_dim.3.gain_ref = f32[1,3584]{1,0:T(1,128)} reshape(f32[3584]{0:T(1024)} %param.10) | data formatting | bytes 28672 | tf_op jit(solution)/shard_map/broadcast_in_dim | solution.py:508
  1.3 1.4 %copy.9.routes_ref = s32[64,8]{1,0:T(8,128)} copy(s32[64,8]{0,1:T(8,128)} %param.12) | data formatting | bytes 4096 | tf_op args[4]
  2.7 109.0 %shard_map.82 = bf16[64,3584]{1,0:T(8,128)(2,1)} custom-call(bf16[64,3584]{1,0:T(8,128)(2,1)} %residual_ref.1, bf16[64,3584]{1,0:T(8,128)(2,1)} %bitcast.2, f32[1,3584]{1,0:T(1,128)} %broadcast_in_dim.3.gain_ref, f32[16,3584]{1,0:T(8,128)} %bitcast.3, s32[64,8]{1,0:T(8,128)} %copy.9.routes_ref, bf16[1,3584,1024]{2,1,0:T(8,128)(2,1)} %gate_hbm.1, ...), custom_call_target="tpu_custom_call" | custom-call | tf_op jit(solution)/shard_map/pallas_call | solution.py:480
  111.7 1.8 %copy.11 = bf16[64,3584]{1,0:T(8,128)(2,1)} copy(bf16[64,3584]{1,0:T(8,128)(2,1)} %shard_map.82) | data formatting | bytes 917504

commit v3 on v2

--- a/solution.py
+++ b/solution.py
@@ -138,7 +138,7 @@
 ):
     n, width = residual_ref.shape
     experts = router_ref.shape[0]
-    top_count = routes_ref.shape[1]
+    top_count = routes_ref.shape[0]
 
     def block_cols(i):
         return pl.ds(pl.multiple_of(i * QBLOCK, QBLOCK), QBLOCK)
@@ -158,7 +158,7 @@
 
     def scale_block(i, carry):
         cols = block_cols(i)
-        normed = stream_ref[:, cols].astype(jnp.float32) * factor * gain_ref[:, cols]
+        normed = stream_ref[:, cols].astype(jnp.float32) * factor * gain_ref[pl.ds(i, 1), :]
         normed_ref[:, cols] = normed
         scale = (jnp.max(jnp.abs(normed), axis=1, keepdims=True) + epsilon) / scale_limit
         scale = scale.astype(jnp.bfloat16).astype(jnp.float32)
@@ -173,10 +173,17 @@
         precision=lax.Precision.HIGHEST, preferred_element_type=jnp.float32,
     )
     affinity = 1.0 / (1.0 + jnp.exp(-logits))
-    labels = lax.broadcasted_iota(jnp.int32, (n, experts), 1)
-    picked = jnp.zeros((n, experts), jnp.float32)
+    labels = lax.broadcasted_iota(jnp.int32, (experts, n), 0)
+    member = jnp.zeros((experts, n), jnp.float32)
     for k in range(top_count):
-        picked = picked + jnp.where(routes_ref[:, k : k + 1] == labels, affinity, 0.0)
+        member = member + jnp.where(routes_ref[k : k + 1, :] == labels, 1.0, 0.0)
+    unit = lax.broadcasted_iota(jnp.int32, (experts, experts), 0)
+    unit = unit == lax.broadcasted_iota(jnp.int32, (experts, experts), 1)
+    member = lax.dot_general(
+        member, jnp.where(unit, 1.0, 0.0), (((0,), (0,)), ((), ())),
+        preferred_element_type=jnp.float32,
+    )
+    picked = jnp.where(member > 0.5, affinity, 0.0)
     weights = route_scale * picked / jnp.sum(picked, axis=1, keepdims=True)
     spread_ref[...] = jnp.zeros_like(spread_ref)
     for piece in range(3):
@@ -505,7 +512,7 @@
             collective_id=0, has_side_effects=True, vmem_limit_bytes=60 * 1024 * 1024
         ),
     )(
-        residual, head_partials[0], norm_gain[None], router_weight.T, routes,
+        residual, head_partials[0], norm_gain.reshape(-1, QBLOCK), router_weight.T, routes.T,
         expert_gate, expert_up, expert_down,
     )
 

time: 114 us -> 111 us (0.974)
  local copies, waits for them, and re-layouts: 4.52 us -> 1.82 us
    unnamed x2 -> x1, local copies, waits for them, and re-layouts: 3.2 us -> 1.82 us
    broadcast_in_dim x1 -> x0, local copies, waits for them, and re-layouts: 1.32 us -> none  [dense(): norm_gain[None]]
where the time goes in v3:
time: 111 us
  Pallas kernels  109 us (98%)
  local copies, waits for them, and re-layouts  1.82 us (2%)
    pallas_call x1, Pallas kernels, dense(): pl.pallas_call(layer_kernel, out_shape=jax.ShapeDtypeStruct((n, width), b...  109 us

profile of v3, /device:TPU:0, one launch (start us, length us, event | category | flops | bytes accessed | tf_op | source)
XLA Modules:
  0.0 110.8 jit_solution(5706634001718522081)
XLA Ops:
  0.0 108.9 %shard_map.82 = bf16[64,3584]{1,0:T(8,128)(2,1)} custom-call(bf16[64,3584]{1,0:T(8,128)(2,1)} %residual_ref.1, bf16[64,3584]{1,0:T(8,128)(2,1)} %bitcast.4, f32[28,128]{1,0:T(8,128)} %bitcast.6, f32[16,3584]{1,0:T(8,128)} %bitcast.5, s32[8,64]{1,0:T(8,128)} %bitcast.7, bf16[1,3584,1024]{2,1,0:T(8,128)(2,1)} %gate_hbm.1, bf16[1,3584,1024]{2,1,0:T(8,128)(2,1)} %up_hbm.1, ...), custom_call_target="tpu_custom_call" | custom-call | tf_op jit(solution)/shard_map/pallas_call | solution.py:487
  109.0 1.8 %copy.10 = bf16[64,3584]{1,0:T(8,128)(2,1)} copy(bf16[64,3584]{1,0:T(8,128)(2,1)} %shard_map.82) | data formatting | bytes 917504
